TPU v7x, 32 devices: a whole 2x2x4 slice. The times are simulated.
32 devices in a mesh: groups: 2 (over x), aux: 16 (over z, y, core).
Axes of the slice: x: 2, y: 2, z: 4, core: 2. Of those that a mesh axis runs over, the one named last changes fastest.
Arguments:
- blocks: bfloat16 [4096, 4096], P(('groups', 'aux')), parts along dimension 0, may hold values from -0.29882812 to 0.29882812
- right_xform: bfloat16 [4096, 4096], P(('groups', 'aux')), parts along dimension 0, may hold values from -0.59765625 to 0.59765625
- left_xform: bfloat16 [4096, 4096], P(('groups', 'aux')), parts along dimension 0, may hold values from -0.59765625 to 0.59765625
- owner: int32 [4096, 1], P(('groups', 'aux')), parts along dimension 0, may hold values from 0 to 15; in each aligned block of 128 rows (0 to 127, 128 to 255, ...) at most 16 rows name the same one
- tile_slot: int32 [4096], P(('groups', 'aux')), parts along dimension 0, may hold values from 0 to 7
- domain: int32 [4096], P(('groups', 'aux')), parts along dimension 0, may hold values from 0 to 2
- live_count: int32 [32], P(('groups', 'aux')), parts along dimension 0, may hold values from 1 to 128, 1536 in all
- right_vec: float32 [16384], P(('groups', 'aux')), parts along dimension 0, may hold values from -6 to 6
- left_vec: float32 [16384], P(('groups', 'aux')), parts along dimension 0, may hold values from -6 to 6
- occ_energy: float32 [8], P('groups'), parts along dimension 0, may hold values from -0.56 to -0.5
- vir_energy: float32 [4096], P('groups'), parts along dimension 0, may hold values from 0.5 to 3
- omega: float32 [2], P('groups'), parts along dimension 0, may hold values from 1.78 to 1.85
Outputs:
- sigma_right: float32 [16384], P(('groups', 'aux')), parts along dimension 0
- sigma_left: float32 [16384], P(('groups', 'aux')), parts along dimension 0
There are 2 independent parts, one for each index of `groups`. A program takes and returns all parts, laid end to end along the dimension named above; each array names one. Nothing has to cross between parts.
Inputs may be any that keep to these rules, and one draw needn't show every extreme that they name: Among the 128 blocks of one aux device at most 16 share an owner, and on some device exactly 16 do. `live_count`: the counts sum to 1536 and some device has all 128 blocks live; blocks at or past the count are ignored.
All inputs are finite; a program needn't handle non-finite values.
Results may differ from a plain program's by a relative error of at most 0.0024.
Values may be sent and summed in bfloat16 or wider, within the bound.
A program may use at most 128 MiB of HBM per device.

v0:
```python
import math

import jax
import jax.numpy as jnp
from jax import lax
from jax.sharding import PartitionSpec as P

BLK = 64
NVIR = 2048
ADOM_DEV = 3


def on_device(
    blocks,
    right_xform,
    left_xform,
    owner,
    tile_slot,
    domain,
    live_count,
    right_vec,
    left_vec,
    occ_energy,
    vir_energy,
    omega,
):
    n_devices = lax.axis_size("aux")
    device = lax.axis_index("aux")
    nb_local = blocks.shape[0]
    block_width = BLK
    flat_width = blocks.shape[1]
    own_pairs = right_vec.shape[0]
    own_tiles = own_pairs // block_width
    domains = ADOM_DEV * n_devices
    capacity = 2 * nb_local // n_devices
    block_ids = jnp.arange(nb_local, dtype=jnp.int32)
    is_live = block_ids < live_count[0]
    combined = jnp.stack([blocks, right_xform, left_xform], axis=1)
    masked3 = jnp.where(is_live[:, None, None], combined, jnp.zeros_like(combined))
    masked_flat = masked3[:, 0]
    target = owner[:, 0]
    onehot = (target[:, None] == jnp.arange(n_devices, dtype=jnp.int32)[None, :]).astype(jnp.int32)
    send_rank = jnp.sum((jnp.cumsum(onehot, axis=0) - onehot) * onehot, axis=1)
    send_slot = target * capacity + send_rank
    global_dom = device * ADOM_DEV + domain
    block_codes = global_dom * own_tiles + tile_slot
    outgoing = (
        jnp.zeros((n_devices * capacity, 3, flat_width), jnp.bfloat16).at[send_slot].set(masked3)
    )
    out_codes = jnp.zeros((n_devices * capacity,), jnp.int32).at[send_slot].set(block_codes)
    arrived, arrived_codes = (
        lax.all_to_all(
            outgoing.reshape(n_devices, capacity, 3, flat_width),
            "aux",
            split_axis=0,
            concat_axis=0,
            tiled=True,
        ),
        lax.all_to_all(
            out_codes.reshape(n_devices, capacity), "aux", split_axis=0, concat_axis=0, tiled=True
        ),
    )
    arrived_b = arrived.reshape(-1, 3, block_width, block_width)
    arrived_codes = arrived_codes.reshape(-1)
    arrived_dom = arrived_codes // own_tiles
    arrived_tile = arrived_codes % own_tiles
    dom_group = math.gcd(domains, 16)
    group_count = domains // dom_group
    group_rows = dom_group * block_width

    def assemble(group_id):
        inside = arrived_dom // dom_group == group_id
        segment_ids = jnp.where(
            inside,
            (arrived_dom - group_id * dom_group) * own_tiles + arrived_tile,
            dom_group * own_tiles,
        )
        slab_piece = jax.ops.segment_sum(
            arrived_b.astype(jnp.float32), segment_ids, num_segments=dom_group * own_tiles + 1
        )[:-1]
        slab_piece = slab_piece.reshape(
            dom_group, own_tiles, 3, block_width, block_width
        ).transpose(2, 0, 3, 1, 4)
        return slab_piece.reshape(3, group_rows, own_pairs)

    masked = masked_flat.reshape(nb_local, block_width, block_width)
    trials = jnp.stack([right_vec, left_vec]).astype(jnp.bfloat16)
    gathered = lax.all_gather(trials, "aux", axis=1, tiled=True)
    picked = gathered.reshape(2, -1, block_width)[:, target * own_tiles + tile_slot, :]
    contrib = jnp.einsum("brc,kbc->kbr", masked, picked, preferred_element_type=jnp.float32)
    pick_dom = (domain[:, None] == jnp.arange(ADOM_DEV, dtype=jnp.int32)[None, :]).astype(
        jnp.float32
    )
    local_sum = jnp.einsum("bd,kbr->kdr", pick_dom, contrib, precision=lax.Precision.HIGHEST)
    coulomb = lax.all_gather(
        local_sum.reshape(2, ADOM_DEV * block_width), "aux", axis=1, tiled=True
    )

    def accumulate(state, group_id):
        cross_sum, coulomb_term = state
        pieces = assemble(group_id)
        slab_piece = pieces[0]
        part_y = lax.dynamic_slice_in_dim(coulomb, group_id * group_rows, group_rows, 1)
        rounded = slab_piece.astype(jnp.bfloat16)
        xform_r = pieces[1].astype(jnp.bfloat16)
        xform_l = pieces[2].astype(jnp.bfloat16)
        contract = (((0,), (0,)), ((), ()))
        product = lax.dot_general(
            rounded,
            jnp.concatenate([xform_r, xform_l], axis=1),
            contract,
            preferred_element_type=jnp.float32,
        )
        coulomb_term = coulomb_term + jnp.dot(part_y, slab_piece, precision=lax.Precision.HIGHEST)
        return ((cross_sum + product, coulomb_term), None)

    start_state = (
        jnp.zeros((own_pairs, 2 * own_pairs), jnp.float32),
        jnp.zeros((2, own_pairs), jnp.float32),
    )
    (cross_sum, coulomb_term), _ = lax.scan(
        accumulate, start_state, jnp.arange(group_count, dtype=jnp.int32)
    )
    cross_right = cross_sum[:, :own_pairs]
    cross_left = cross_sum[:, own_pairs:]
    gram_right = cross_right + cross_right.T
    first_pair = device * own_pairs
    occ_index = first_pair // NVIR
    vir_start = first_pair % NVIR
    energy_gap = lax.dynamic_slice_in_dim(
        vir_energy, vir_start, own_pairs
    ) - lax.dynamic_slice_in_dim(occ_energy, occ_index, 1)
    denominator = omega[0] - energy_gap[:, None] - energy_gap[None, :]
    sigma_right = (
        energy_gap * right_vec
        + coulomb_term[0]
        + jnp.dot(gram_right / denominator, right_vec, precision=lax.Precision.HIGHEST)
    )
    sigma_left = (
        energy_gap * left_vec
        + coulomb_term[1]
        + jnp.dot(cross_left / denominator, left_vec, precision=lax.Precision.HIGHEST)
    )
    return (sigma_right, sigma_left)


def solution(mesh):
    in_specs = (
        P(("groups", "aux"), None),
        P(("groups", "aux"), None),
        P(("groups", "aux"), None),
        P(("groups", "aux"), None),
        P(("groups", "aux")),
        P(("groups", "aux")),
        P(("groups", "aux")),
        P(("groups", "aux")),
        P(("groups", "aux")),
        P("groups"),
        P("groups"),
        P("groups"),
    )
    out_specs = (P(("groups", "aux")), P(("groups", "aux")))
    return jax.shard_map(
        on_device, mesh=mesh, in_specs=in_specs, out_specs=out_specs, check_vma=False
    )
```

profile of v0, /device:TPU:1, one launch (start us, length us, event | category | flops | bytes accessed | tf_op | source)
XLA Modules:
  0.0 708.8 jit_solution(1650772573321471088)
XLA Ops:
  5.5 7.3 %all-to-all-start = ((s32[16,1,16]{2,1,0:T(1,128)}), s32[16,1,16]{2,1,0:T(1,128)S(1)}, u32[]{:S(2)}, u32[]{:S(2)}) async-start(s32[16,1,16]{2,1,0:T(1,128)} %all_to_all.9), calls=%async_computation | async-start | bytes 16384 | tf_op jit(solution)/shard_map/all_to_all | solution.py:59
  26.9 7.5 %broadcast_in_dim.45 = bf16[256,3,4096]{2,1,0:T(4,128)(2,1)} broadcast(bf16[]{:T(256)} %constant.155.clone.1), dimensions={} | broadcast | bytes 6291458 | tf_op jit(solution)/shard_map/broadcast_in_dim | solution.py:48
  34.4 19.7 %scatter_fusion.1 = bf16[256,3,4096]{2,1,0:T(4,128)(2,1)} fusion(bf16[256,3,4096]{2,1,0:T(4,128)(2,1)} %broadcast_in_dim.45, s32[128]{0:T(128)S(1)} %fusion.22, bf16[128,3,4096]{2,1,0:T(4,128)(2,1)} %copy.47), kind=kCustom, calls=%fused_computation.3 | custom fusion | bytes 9437696 | tf_op jit(solution)/shard_map/scatter | solution.py:48
  54.1 11.1 %copy.48 = bf16[16,16,3,4096]{3,1,2,0:T(8,128)(2,1)} copy(bf16[16,16,3,4096]{3,2,1,0:T(4,128)(2,1)} %bitcast.77) | data formatting | bytes 12582912 | tf_op jit(solution)/shard_map/reshape | solution.py:53
  65.2 6.5 all-to-all-start.1
  76.9 112.7 %all_gather.6 = bf16[2,8192]{1,0:T(2,128)(2,1)S(1)} all-gather(bf16[2,512]{1,0:T(2,128)(2,1)S(1)} %pad_maximum_fusion), channel_id=1, replica_groups=mesh['groups'=2,'aux'=16] {'aux'}, dimensions={1}, use_global_device_ids=true | all-gather | bytes 34816 | tf_op jit(solution)/shard_map/all_gather | solution.py:88
  192.0 49.4 %all-gather = f32[16,192,2]{1,2,0:T(2,128)S(1)} all-gather(f32[1,192,2]{1,2,0:T(2,128)S(1)} %bitcast.87), channel_id=1, replica_groups=mesh['groups'=2,'aux'=16] {'aux'}, dimensions={0}, use_global_device_ids=true | all-gather | bytes 26112 | tf_op jit(solution)/shard_map/all_gather | solution.py:95
  246.4 11.5 %copy.57 = bf16[16,16,3,4096]{3,2,1,0:T(4,128)(2,1)} copy(bf16[16,16,3,4096]{3,1,2,0:T(8,128)(2,1)} %all-to-all-done.1) | data formatting | bytes 12582912
  257.9 22.6 %reshape.248 = bf16[256,3,64,64]{3,2,1,0:T(8,128)(2,1)} reshape(bf16[16,16,3,4096]{3,2,1,0:T(4,128)(2,1)} %copy.57) | data formatting | bytes 12582912
  280.5 418.8 %while.16 = (s32[]{:T(128)}, f32[512,1024]{1,0:T(8,128)}, f32[2,512]{1,0:T(2,128)S(1)}, s32[256,1]{0,1:T(1,128)S(1)}, s32[256]{0:T(256)S(1)}, /*index=5*/s32[256...) while((s32[]{:T(128)}, f32[512,1024]{1,0:T(8,128)}, ...), condition=%wide.region_6.7_spmd.clone, body=%wide.region_4.6_spmd.clone.sunk | while | flops 1099962880 | bytes 120658176 | solution.py:121
  296.1 14.5 %convert_element_type.50 = f32[256,3,64,64]{3,2,1,0:T(8,128)} convert(bf16[256,3,64,64]{3,2,1,0:T(8,128)(2,1)} %get-tuple-element.348) | non-fusion elementwise | flops 3145728 | bytes 18874368 | tf_op jit(solution)/shard_map/while/body/eval_jaxpr/convert_element_type | solution.py:79
  310.6 6.2 broadcast.270
  316.9 63.4 %scatter_fusion = f32[129,3,64,64]{3,2,1,0:T(8,128)} fusion(f32[129,3,64,64]{3,2,1,0:T(8,128)} %broadcast.270, s32[256]{0:T(256)S(1)} %bitcast.83, f32[256,3,64,64]{3,2,1,0:T(8,128)} %convert_element_type.50), kind=kCustom, calls=%fused_computation.1.clone.clone.1 | custom fusion | flops 3145728 | bytes 37749760 | tf_op jit(solution)/shard_map/while/body/eval_jaxpr/scatter-add | solution.py:78
  380.3 11.8 %slice.81 = f32[128,3,64,64]{3,2,1,0:T(8,128)} slice(f32[129,3,64,64]{3,2,1,0:T(8,128)} %scatter_fusion), slice={[0:128], [0:3], [0:64], [0:64]} | slice | bytes 12582912 | tf_op jit(solution)/shard_map/while/body/eval_jaxpr/slice | solution.py:78
  392.1 6.3 convert.26
  428.0 14.5 %convert_element_type.50 = f32[256,3,64,64]{3,2,1,0:T(8,128)} convert(bf16[256,3,64,64]{3,2,1,0:T(8,128)(2,1)} %get-tuple-element.348) | non-fusion elementwise | flops 3145728 | bytes 18874368 | tf_op jit(solution)/shard_map/while/body/eval_jaxpr/convert_element_type | solution.py:79
  448.8 67.2 %scatter_fusion = f32[129,3,64,64]{3,2,1,0:T(8,128)} fusion(f32[129,3,64,64]{3,2,1,0:T(8,128)} %broadcast.270, s32[256]{0:T(256)S(1)} %bitcast.83, f32[256,3,64,64]{3,2,1,0:T(8,128)} %convert_element_type.50), kind=kCustom, calls=%fused_computation.1.clone.clone.1 | custom fusion | flops 3145728 | bytes 37749760 | tf_op jit(solution)/shard_map/while/body/eval_jaxpr/scatter-add | solution.py:78
  515.9 11.8 %slice.81 = f32[128,3,64,64]{3,2,1,0:T(8,128)} slice(f32[129,3,64,64]{3,2,1,0:T(8,128)} %scatter_fusion), slice={[0:128], [0:3], [0:64], [0:64]} | slice | bytes 12582912 | tf_op jit(solution)/shard_map/while/body/eval_jaxpr/slice | solution.py:78
  527.8 6.3 convert.26
  564.4 14.5 %convert_element_type.50 = f32[256,3,64,64]{3,2,1,0:T(8,128)} convert(bf16[256,3,64,64]{3,2,1,0:T(8,128)(2,1)} %get-tuple-element.348) | non-fusion elementwise | flops 3145728 | bytes 18874368 | tf_op jit(solution)/shard_map/while/body/eval_jaxpr/convert_element_type | solution.py:79
  578.9 6.2 broadcast.270
  585.1 67.7 %scatter_fusion = f32[129,3,64,64]{3,2,1,0:T(8,128)} fusion(f32[129,3,64,64]{3,2,1,0:T(8,128)} %broadcast.270, s32[256]{0:T(256)S(1)} %bitcast.83, f32[256,3,64,64]{3,2,1,0:T(8,128)} %convert_element_type.50), kind=kCustom, calls=%fused_computation.1.clone.clone.1 | custom fusion | flops 3145728 | bytes 37749760 | tf_op jit(solution)/shard_map/while/body/eval_jaxpr/scatter-add | solution.py:78
  652.9 11.8 %slice.81 = f32[128,3,64,64]{3,2,1,0:T(8,128)} slice(f32[129,3,64,64]{3,2,1,0:T(8,128)} %scatter_fusion), slice={[0:128], [0:3], [0:64], [0:64]} | slice | bytes 12582912 | tf_op jit(solution)/shard_map/while/body/eval_jaxpr/slice | solution.py:78
  664.7 6.3 convert.26
  (111 shorter events, 131.4 us)
Async XLA Ops:
  0.6 16.8 %copy-start.2 = (bf16[128,4096]{1,0:T(8,128)(2,1)S(1)}, bf16[128,4096]{1,0:T(8,128)(2,1)}, u32[]{:S(2)}) copy-start(bf16[128,4096]{1,0:T(8,128)(2,1)} %param.14) | copy-start | bytes 3145732
  5.5 59.7 %all-to-all-start = ((s32[16,1,16]{2,1,0:T(1,128)}), s32[16,1,16]{2,1,0:T(1,128)S(1)}, u32[]{:S(2)}, u32[]{:S(2)}) async-start(s32[16,1,16]{2,1,0:T(1,128)} %all_to_all.9), calls=%async_computation | async-start | bytes 16384 | tf_op jit(solution)/shard_map/all_to_all | solution.py:59
  65.2 181.2 %all-to-all-start.1 = ((bf16[16,16,3,4096]{3,1,2,0:T(8,128)(2,1)}), bf16[16,16,3,4096]{3,1,2,0:T(8,128)(2,1)}, u32[]{:S(2)}, u32[]{:S(2)}) async-start(bf16[16,16,3,4096]{3,1,2,0:T(8,128)(2,1)} %copy.48), calls=%async_computation.1 | async-start | bytes 12582912 | tf_op jit(solution)/shard_map/all_to_all | solution.py:52
  71.7 5.1 copy-start.4
  71.7 5.1 copy-start.6
  72.8 118.9 %copy-start.9 = (s32[128]{0:T(128)S(1)}, s32[128]{0:T(128)}, u32[]{:S(2)}) copy-start(s32[128]{0:T(128)} %param.19) | copy-start | bytes 1540
  72.8 169.4 %copy-start.11 = (f32[4]{0:T(128)S(1)}, f32[4]{0:T(128)}, u32[]{:S(2)}) copy-start(f32[4]{0:T(128)} %param.23) | copy-start | bytes 52
  702.2 2.8 copy-start
  702.2 2.8 copy-start.5
  702.2 2.8 copy-start.8
  702.2 2.8 copy-start.10
  703.6 2.5 copy-start.7
  705.0 1.6 copy-start.1
  705.0 1.9 copy-start.3
where the time goes:
time: 717 us; the launch traced here: 709 us
  other arithmetic  271 us (38%)
  local copies, waits for them, and re-layouts  221 us (31%)
  blocking collectives  162 us (23%)
  matrix products  19.8 us (3%)
  loops' own time  17.9 us (2%)
  starting transfers between devices  13.8 us (2%)
    scatter-add x3, other arithmetic, assemble(): jax.ops.segment_sum(arrived_b.astype(jnp.float32), segment_ids, num_segme...  198 us
    all_gather x1, blocking collectives, on_device(): gathered = lax.all_gather(trials, 'aux', axis=1, tiled=True)  113 us
    all_gather x1, blocking collectives, on_device(): lax.all_gather(local_sum.reshape(2, ADOM_DEV * block_width), 'aux', axis=...  49.4 us
    convert_element_type x3, other arithmetic, assemble(): arrived_b.astype(jnp.float32)  43.5 us
    unnamed x30, local copies, waits for them, and re-layouts  40.8 us
    slice x3, local copies, waits for them, and re-layouts, assemble(): jax.ops.segment_sum(arrived_b.astype(jnp.float32), segment_ids, num_segme...  35.5 us
    slice x6, local copies, waits for them, and re-layouts, accumulate(): slab_piece = pieces[0]  23.2 us
    scatter x1, local copies, waits for them, and re-layouts, on_device(): jnp.zeros((n_devices * capacity, 3, flat_width), jnp.bfloat16).at[send_slot]  19.7 us
  transfers between devices with their start and end apart: 2, of which 0 were waited for; matrix products, arithmetic and copies ran while one was open for 9% of the time, Pallas kernels for 0%

commit v1 on v0

v1 whole, which is shorter than its diff:
```python
import functools

import jax
import jax.numpy as jnp
from jax import lax
from jax.experimental import pallas as pl
from jax.experimental.pallas import tpu as pltpu
from jax.sharding import PartitionSpec as P

BLK = 64
NVIR = 2048
ADOM_DEV = 3
LANES = 128
F32 = jnp.float32
BF16 = jnp.bfloat16


def kernel(
    n,
    group,
    occ_ref,
    omega_ref,
    code_ref,
    blocks_ref,
    right_ref,
    left_ref,
    trial_ref,
    vir_ref,
    out_ref,
    b_slab,
    r_slab,
    l_slab,
    vir_col,
    w_right,
    w_left,
    y_ref,
    trials,
    share,
    arrived,
    gather_send,
    gather_recv,
    share_send,
    share_recv,
):
    me = lax.axis_index("aux")
    pairs = w_right.shape[0]
    lane_tiles = pairs // LANES
    rows_of_slab = ADOM_DEV * lane_tiles
    sub = BLK * BLK // LANES
    slab_rows = ADOM_DEV * BLK
    hot_rows = group * rows_of_slab

    def peer(step):
        return lax.rem(me + 1 + step, n)

    barrier = pltpu.get_barrier_semaphore()

    def greet(step, carry):
        pl.semaphore_signal(barrier, inc=1, device_id={"aux": peer(step)})
        return carry

    lax.fori_loop(0, n - 1, greet, 0)
    pl.semaphore_wait(barrier, n - 1)

    def gather_copy(target, source):
        return pltpu.make_async_remote_copy(
            src_ref=trial_ref,
            dst_ref=trials.at[source],
            send_sem=gather_send.at[target],
            recv_sem=gather_recv.at[source],
            device_id={"aux": target},
        )

    def share_copy(target, source):
        return pltpu.make_async_remote_copy(
            src_ref=share.at[target],
            dst_ref=arrived.at[source],
            send_sem=share_send.at[target],
            recv_sem=share_recv.at[source],
            device_id={"aux": target},
        )

    def start_gather(step, carry):
        gather_copy(peer(step), me).start()
        return carry

    lax.fori_loop(0, n - 1, start_gather, 0)
    trials[me] = trial_ref[...]

    for i in range(NVIR // LANES):
        row = jnp.broadcast_to(vir_ref[i : i + 1, :], (LANES, LANES))
        vir_col[i * LANES : (i + 1) * LANES, :] = row.T

    def assemble(source_ref, slab, base, g):
        slot = lax.broadcasted_iota(jnp.int32, (hot_rows, code_ref.shape[1]), 0)
        hot = jnp.where(slot + g * hot_rows == code_ref[...], 1.0, 0.0).astype(BF16)
        low = lax.broadcasted_iota(jnp.int32, (source_ref.shape[0], LANES), 1) < BLK

        def chunk(j, carry):
            straight, crossed = [], []
            for half in range(2):
                x = source_ref[:, pl.ds(pl.multiple_of(j * 2 * LANES + half * LANES, LANES), LANES)]
                x = x.astype(F32)
                turned = pltpu.roll(x, BLK, 1)
                zero = jnp.zeros_like(x)
                straight.append(
                    jnp.concatenate([jnp.where(low, x, zero), jnp.where(low, zero, turned)], 0)
                )
                crossed.append(
                    jnp.concatenate([jnp.where(low, turned, zero), jnp.where(low, zero, x)], 0)
                )
            for parity, parts in enumerate((straight, crossed)):
                z = jnp.concatenate(parts, 1).astype(BF16)
                placed = jnp.dot(hot, z, preferred_element_type=F32)
                for half in range(2):
                    slab[parity, pl.ds(base + j * 2 + half, hot_rows, stride=sub), :] = placed[
                        :, half * LANES : (half + 1) * LANES
                    ]
            return carry

        lax.fori_loop(0, sub // 2, chunk, 0)

    def lane_tile(slab, s, t):
        parts = []
        for d in range(ADOM_DEV):
            for parity in range(2):
                first = (s * rows_of_slab + d * lane_tiles + t) * sub
                parts.append(slab[parity, pl.ds(pl.multiple_of(first, sub), sub), :])
        return jnp.concatenate(parts, 0)

    for g in range(n // group):
        assemble(blocks_ref, b_slab, g * hot_rows * sub, g)

    def wait_gather(step, carry):
        gather_copy(peer(step), peer(step)).wait_recv()
        return carry

    lax.fori_loop(0, n - 1, wait_gather, 0)

    def add_y(s, state):
        acc_r, acc_l = state
        vec = trials[s].astype(BF16).astype(F32)
        for t in range(lane_tiles):
            tile = lane_tile(b_slab, s, t)
            acc_r = acc_r + tile * vec[t : t + 1, :]
            acc_l = acc_l + tile * vec[lane_tiles + t : lane_tiles + t + 1, :]
        return acc_r, acc_l

    zero = jnp.zeros((slab_rows, LANES), F32)
    acc_r, acc_l = lax.fori_loop(0, n, add_y, (zero, zero))
    y_ref[0] = jnp.broadcast_to(jnp.sum(acc_r, 1, keepdims=True), (slab_rows, LANES))
    y_ref[1] = jnp.broadcast_to(jnp.sum(acc_l, 1, keepdims=True), (slab_rows, LANES))

    per_occ = NVIR // pairs
    nt = (((1,), (1,)), ((), ()))

    for g in range(n // group):
        assemble(right_ref, r_slab, 0, g)
        assemble(left_ref, l_slab, 0, g)

        def slab_step(step, carry):
            local = lax.rem(me + 1 + step, group)
            s = g * group + local
            shift = omega_ref[0] + 2.0 * occ_ref[s // per_occ]
            part = lax.rem(s, per_occ)
            column = vir_col[pl.ds(pl.multiple_of(part * pairs, pairs), pairs), :]
            energies = vir_ref[pl.ds(part * lane_tiles, lane_tiles), :]
            vec = trials[s]
            for t in range(lane_tiles):
                lanes = slice(t * LANES, (t + 1) * LANES)
                inverse = pl.reciprocal((shift - energies[t : t + 1, :]) - column, approx=True)
                w_right[:, lanes] = (inverse * vec[t : t + 1, :]).astype(BF16)
                w_left[:, lanes] = (
                    inverse * vec[lane_tiles + t : lane_tiles + t + 1, :]
                ).astype(BF16)
            b = jnp.concatenate([lane_tile(b_slab, s, t) for t in range(lane_tiles)], 1)
            x_r = jnp.concatenate([lane_tile(r_slab, local, t) for t in range(lane_tiles)], 1)
            x_l = jnp.concatenate([lane_tile(l_slab, local, t) for t in range(lane_tiles)], 1)
            b16, r16 = b.astype(BF16), x_r.astype(BF16)
            t_r = lax.dot_general(r16, w_right[...], nt, preferred_element_type=F32)
            t_b = lax.dot_general(b16, w_right[...], nt, preferred_element_type=F32)
            t_l = lax.dot_general(x_l.astype(BF16), w_left[...], nt, preferred_element_type=F32)
            y_r = jnp.concatenate([y_ref[0]] * lane_tiles, 1)
            y_l = jnp.concatenate([y_ref[1]] * lane_tiles, 1)
            sig_r = jnp.sum(b * (t_r + y_r) + x_r * t_b, 0, keepdims=True)
            sig_l = jnp.sum(b * (t_l + y_l), 0, keepdims=True)
            for t in range(lane_tiles):
                lanes = slice(t * LANES, (t + 1) * LANES)
                share[s, t : t + 1, :] = sig_r[:, lanes]
                share[s, lane_tiles + t : lane_tiles + t + 1, :] = sig_l[:, lanes]

            @pl.when(s != me)
            def _():
                share_copy(s, me).start()

            return carry

        lax.fori_loop(0, group, slab_step, 0)

    own = lax.rem(me, per_occ)
    energies = vir_ref[pl.ds(own * lane_tiles, lane_tiles), :] - occ_ref[me // per_occ]
    total = jnp.concatenate([energies, energies], 0) * trial_ref[...] + share[me]

    def collect(step, total):
        source = peer(step)
        share_copy(source, source).wait_recv()
        return total + arrived[source]

    out_ref[...] = lax.fori_loop(0, n - 1, collect, total)

    def wait_sent(step, carry):
        gather_copy(peer(step), me).wait_send()
        share_copy(peer(step), me).wait_send()
        return carry

    lax.fori_loop(0, n - 1, wait_sent, 0)


def on_device(
    blocks,
    right_xform,
    left_xform,
    owner,
    tile_slot,
    domain,
    live_count,
    right_vec,
    left_vec,
    occ_energy,
    vir_energy,
    omega,
):
    n = lax.axis_size("aux")
    nb_local, flat_width = blocks.shape
    pairs = right_vec.shape[0]
    lane_tiles = pairs // LANES
    group = min(n, 16)
    is_live = jnp.arange(nb_local, dtype=jnp.int32) < live_count[0]
    slot = (owner[:, 0] * ADOM_DEV + domain) * lane_tiles + tile_slot // 2
    code = jnp.concatenate(
        [jnp.where(is_live & (tile_slot % 2 == half), slot, -1) for half in range(2)]
    )[None, :]
    trial = jnp.concatenate([right_vec, left_vec]).reshape(2 * lane_tiles, LANES)
    vir = vir_energy.reshape(NVIR // LANES, LANES)
    sub = flat_width // LANES
    slab = group * ADOM_DEV * lane_tiles * sub
    vmem, smem = (
        pl.BlockSpec(memory_space=pltpu.VMEM),
        pl.BlockSpec(memory_space=pltpu.SMEM),
    )
    out = pl.pallas_call(
        functools.partial(kernel, n, group),
        out_shape=jax.ShapeDtypeStruct((2 * lane_tiles, LANES), F32),
        in_specs=[smem, smem] + [vmem] * 6,
        out_specs=vmem,
        scratch_shapes=[
            pltpu.VMEM((2, slab * (n // group), LANES), F32),
            pltpu.VMEM((2, slab, LANES), F32),
            pltpu.VMEM((2, slab, LANES), F32),
            pltpu.VMEM((NVIR, LANES), F32),
            pltpu.VMEM((pairs, pairs), BF16),
            pltpu.VMEM((pairs, pairs), BF16),
            pltpu.VMEM((2, ADOM_DEV * BLK, LANES), F32),
            pltpu.VMEM((n, 2 * lane_tiles, LANES), F32),
            pltpu.VMEM((n, 2 * lane_tiles, LANES), F32),
            pltpu.VMEM((n, 2 * lane_tiles, LANES), F32),
            pltpu.SemaphoreType.DMA((n,)),
            pltpu.SemaphoreType.DMA((n,)),
            pltpu.SemaphoreType.DMA((n,)),
            pltpu.SemaphoreType.DMA((n,)),
        ],
        compiler_params=pltpu.CompilerParams(
            collective_id=0, has_side_effects=True, vmem_limit_bytes=56 * 1024 * 1024
        ),
    )(occ_energy, omega, code, blocks, right_xform, left_xform, trial, vir)
    return out[:lane_tiles].reshape(pairs), out[lane_tiles:].reshape(pairs)


def solution(mesh):
    in_specs = (
        P(("groups", "aux"), None),
        P(("groups", "aux"), None),
        P(("groups", "aux"), None),
        P(("groups", "aux"), None),
        P(("groups", "aux")),
        P(("groups", "aux")),
        P(("groups", "aux")),
        P(("groups", "aux")),
        P(("groups", "aux")),
        P("groups"),
        P("groups"),
        P("groups"),
    )
    out_specs = (P(("groups", "aux")), P(("groups", "aux")))
    return jax.shard_map(
        on_device, mesh=mesh, in_specs=in_specs, out_specs=out_specs, check_vma=False
    )
```

time: 717 us -> 54.9 us (0.08); the launches traced: 709 us -> 54.7 us
  other arithmetic: 271 us -> 1.19 us
  local copies, waits for them, and re-layouts: 221 us -> 2.11 us
  blocking collectives: 162 us -> 0 us
  Pallas kernels: 0 us -> 49.4 us
  matrix products: 19.8 us -> 0 us
  loops' own time: 17.9 us -> 0 us
  starting transfers between devices: 13.8 us -> 0 us
    scatter-add x3 -> x0, other arithmetic: 198 us -> none  [assemble(): jax.ops.segment_sum(arrived_b.astype(jnp.float32), segment_ids, num_segme...]
    all_gather x2 -> x0, blocking collectives: 162 us -> none  [the longest x1 113 us: on_device(): gathered = lax.all_gather(trials, 'aux', axis=1, tiled=True)]
    slice x22 -> x0, local copies, waits for them, and re-layouts: 84.8 us -> none  [the longest x3 35.5 us: assemble(): jax.ops.segment_sum(arrived_b.astype(jnp.float32), segment_ids, num_segme...]
    pallas_call x0 -> x1, Pallas kernels: none -> 49.4 us  [on_device(): pl.pallas_call(functools.partial(kernel, n, group), out_shape=jax.ShapeDt...]
    convert_element_type x4 -> x0, other arithmetic: 44.3 us -> none  [the longest x3 43.5 us: assemble(): arrived_b.astype(jnp.float32)]
    unnamed x30 -> x10, local copies, waits for them, and re-layouts: 40.8 us -> 0.77 us
    another operation x6 -> x0, local copies, waits for them, and re-layouts: 22.7 us -> none
    scatter x2 -> x0, local copies, waits for them, and re-layouts: 20.7 us -> none  [the longest x1 19.7 us: on_device(): jnp.zeros((n_devices * capacity, 3, flat_width), jnp.bfloat16).at[send_slot]]
  transfers between devices with their start and end apart: 2 -> 0, of which waited for: 0 -> 0; matrix products, arithmetic and copies ran while one was open for 9% -> 0% of each run, Pallas kernels for 0% -> 0%
where the time goes in v1:
time: 54.9 us; the launch traced here: 54.7 us
  Pallas kernels  49.4 us (90%)
  local copies, waits for them, and re-layouts  2.11 us (4%)
  between operations  1.98 us (4%)
  other arithmetic  1.19 us (2%)
    pallas_call x1, Pallas kernels, on_device(): pl.pallas_call(functools.partial(kernel, n, group), out_shape=jax.ShapeDt...  49.4 us
    reshape x1, local copies, waits for them, and re-layouts, on_device(): return (out[:lane_tiles].reshape(pairs), out[lane_tiles:].reshape(pairs))  1.33 us

profile of v1, /device:TPU:1, one launch (start us, length us, event | category | flops | bytes accessed | tf_op | source)
XLA Modules:
  0.0 54.7 jit_solution(6501783340308643075)
XLA Ops:
  1.9 0.0 copy-start.2
  1.9 0.0 copy-start.3
  1.9 0.0 copy-start.4
  2.0 0.6 %copy-done.2 = s32[128]{0:T(128)S(1)} copy-done((s32[128]{0:T(128)S(1)}, s32[128]{0:T(128)}, u32[]{:S(2)}) %copy-start.2) | copy-done | bytes 536
  2.6 0.0 copy-done.3
  2.6 0.0 copy-done.4
  2.6 0.0 copy-start.1
  2.7 0.0 copy-start
  2.7 0.6 %pad_add_fusion = s32[256]{0:T(256)} fusion(s32[128]{0:T(128)S(1)} %and_select_fusion, s32[128]{0:T(128)S(1)} %get-tuple-element.2), kind=kLoop, calls=%fused_computation.10 | loop fusion | flops 256 | bytes 2048 | tf_op jit(solution)/shard_map/concatenate | solution.py:240
  3.2 0.1 copy-done.1
  3.3 0.0 copy-done
  3.3 0.6 %pad_maximum_fusion.trial_ref = f32[8,128]{1,0:T(8,128)} fusion(f32[4,128]{1,0:T(4,128)S(1)} %bitcast.20, f32[4,128]{1,0:T(4,128)S(1)} %bitcast.21), kind=kLoop, calls=%fused_computation | loop fusion | flops 1024 | bytes 8192 | tf_op jit(solution)/shard_map/concatenate | solution.py:243
  3.9 49.4 %shard_map.131 = f32[8,128]{1,0:T(8,128)} custom-call(f32[4]{0:T(128)} %occ_ref.1, f32[1]{0:T(128)S(6)} %copy.15.omega_ref, s32[1,256]{1,0:T(1,128)} %bitcast.19, bf16[128,4096]{1,0:T(8,128)(2,1)} %blocks_ref.1, bf16[128,4096]{1,0:T(8,128)(2,1)} %right_ref.1, bf16[128,4096]{1,0:T(8,128)(2,1)} %left_ref.1, f32[8,128]{1,0:T(8,128)} %pad_maximum_fusion.trial_ref, ...), custom_call_target="tpu_custom_call" | custom-call | tf_op jit(solution)/shard_map/pallas_call | solution.py:251
  53.4 1.3 %slice_bitcast_fusion = (f32[512]{0:T(512)}, f32[512]{0:T(512)}) fusion(f32[8,128]{1,0:T(8,128)} %shard_map.131), kind=kLoop, calls=%fused_computation.1 | loop fusion | bytes 8192 | tf_op jit(solution)/shard_map/reshape | solution.py:276
  (2 shorter events, 0.0 us)
Async XLA Ops:
  1.9 0.7 %copy-start.2 = (s32[128]{0:T(128)S(1)}, s32[128]{0:T(128)}, u32[]{:S(2)}) copy-start(s32[128]{0:T(128)} %param.16) | copy-start | bytes 1540
  1.9 0.7 %copy-start.3 = (s32[128]{0:T(128)S(1)}, s32[128]{0:T(128)}, u32[]{:S(2)}) copy-start(s32[128]{0:T(128)} %param.17) | copy-start | bytes 1540
  1.9 0.7 %copy-start.4 = (s32[128,1]{0,1:T(1,128)S(1)}, s32[128,1]{0,1:T(1,128)}, u32[]{:S(2)}) copy-start(s32[128,1]{0,1:T(1,128)} %param.15) | copy-start | bytes 1540
  2.6 0.7 %copy-start.1 = (f32[512]{0:T(512)S(1)}, f32[512]{0:T(512)}, u32[]{:S(2)}) copy-start(f32[512]{0:T(512)} %param.19) | copy-start | bytes 6148
  2.7 0.7 %copy-start = (f32[512]{0:T(512)S(1)}, f32[512]{0:T(512)}, u32[]{:S(2)}) copy-start(f32[512]{0:T(512)} %param.20) | copy-start | bytes 6148

commit v2 on v1

v2 whole, which is shorter than its diff:
```python
import functools

import jax
import jax.numpy as jnp
from jax import lax
from jax.experimental import pallas as pl
from jax.experimental.pallas import tpu as pltpu
from jax.sharding import PartitionSpec as P

BLK = 64
NVIR = 2048
ADOM_DEV = 3
LANES = 128
F32 = jnp.float32
BF16 = jnp.bfloat16


def kernel(
    n,
    occ_ref,
    omega_ref,
    block_of_ref,
    code_row_ref,
    code_col_ref,
    blocks_ref,
    right_ref,
    left_ref,
    trial_ref,
    vir_ref,
    out_ref,
    turned,
    b_straight,
    b_crossed,
    r_straight,
    r_crossed,
    l_straight,
    l_crossed,
    vir_col,
    w_right,
    w_left,
    y_ref,
    trials,
    share,
    arrived,
    gather_send,
    gather_recv,
    share_send,
    share_recv,
):
    me = lax.axis_index("aux")
    pairs = w_right.shape[0]
    lane_tiles = pairs // LANES
    tiles = 2 * lane_tiles
    sub = BLK * BLK // LANES
    slab_rows = ADOM_DEV * BLK
    nb = blocks_ref.shape[0]
    pitch = turned.shape[0] // nb

    def peer(step):
        return lax.rem(me + 1 + step, n)

    barrier = pltpu.get_barrier_semaphore()

    def greet(step, carry):
        pl.semaphore_signal(barrier, inc=1, device_id={"aux": peer(step)})
        return carry

    lax.fori_loop(0, n - 1, greet, 0)

    for i in range(NVIR // LANES):
        row = jnp.broadcast_to(vir_ref[i : i + 1, :], (LANES, LANES))
        vir_col[i * LANES : (i + 1) * LANES, :] = row.T

    pl.semaphore_wait(barrier, n - 1)

    def gather_copy(target, source):
        return pltpu.make_async_remote_copy(
            src_ref=trial_ref,
            dst_ref=trials.at[source],
            send_sem=gather_send.at[target],
            recv_sem=gather_recv.at[source],
            device_id={"aux": target},
        )

    def share_copy(target, source):
        return pltpu.make_async_remote_copy(
            src_ref=share.at[target],
            dst_ref=arrived.at[source],
            send_sem=share_send.at[target],
            recv_sem=share_recv.at[source],
            device_id={"aux": target},
        )

    def start_gather(step, carry):
        gather_copy(peer(step), me).start()
        return carry

    lax.fori_loop(0, n - 1, start_gather, 0)
    trials[me] = trial_ref[...]

    same = jnp.where(code_col_ref[...] == code_row_ref[...], 1.0, 0.0).astype(BF16)

    def assemble(source_ref, straight, crossed):
        def chunk(j, carry):
            first = pl.multiple_of(j * 2 * LANES, 2 * LANES)
            merged = jnp.dot(
                same, source_ref[:, pl.ds(first, 2 * LANES)], preferred_element_type=F32
            )
            for half in range(2):
                turned[pl.ds(j * 2 + half, nb, stride=pitch), :] = merged[
                    :, half * LANES : (half + 1) * LANES
                ]
            return carry

        lax.fori_loop(0, sub // 2, chunk, 0)

        def settle(i, carry):
            for k in range(8):
                b = i * 8 + k
                x = turned[pl.ds(pl.multiple_of(b * pitch, 8), sub), :]
                straight[b] = x.astype(BF16)
                crossed[b] = pltpu.roll(x, BLK, 1).astype(BF16)
            return carry

        lax.fori_loop(0, nb // 8, settle, 0)
        straight[nb] = jnp.zeros((sub, LANES), BF16)
        crossed[nb] = jnp.zeros((sub, LANES), BF16)

    low = lax.broadcasted_iota(jnp.int32, (sub, LANES), 1) < BLK

    def lane_tile(straight, crossed, s, t):
        parts = []
        for d in range(ADOM_DEV):
            slot = s * (ADOM_DEV * tiles) + d * tiles + 2 * t
            first, second = block_of_ref[slot], block_of_ref[slot + 1]
            parts.append(jnp.where(low, straight[first], crossed[second]))
            parts.append(jnp.where(low, crossed[first], straight[second]))
        return jnp.concatenate(parts, 0)

    assemble(blocks_ref, b_straight, b_crossed)
    assemble(right_ref, r_straight, r_crossed)
    assemble(left_ref, l_straight, l_crossed)

    def wait_gather(step, carry):
        gather_copy(peer(step), peer(step)).wait_recv()
        return carry

    lax.fori_loop(0, n - 1, wait_gather, 0)

    def add_y(s, state):
        acc_r, acc_l = state
        vec = trials[s].astype(BF16).astype(F32)
        for t in range(lane_tiles):
            tile = lane_tile(b_straight, b_crossed, s, t).astype(F32)
            acc_r = acc_r + tile * vec[t : t + 1, :]
            acc_l = acc_l + tile * vec[lane_tiles + t : lane_tiles + t + 1, :]
        return acc_r, acc_l

    zero = jnp.zeros((slab_rows, LANES), F32)
    acc_r, acc_l = lax.fori_loop(0, n, add_y, (zero, zero))
    y_ref[0] = jnp.broadcast_to(jnp.sum(acc_r, 1, keepdims=True), (slab_rows, LANES))
    y_ref[1] = jnp.broadcast_to(jnp.sum(acc_l, 1, keepdims=True), (slab_rows, LANES))

    per_occ = NVIR // pairs

    def slab_step(step, carry):
        s = peer(step)
        shift = omega_ref[0] + 2.0 * occ_ref[s // per_occ]
        part = lax.rem(s, per_occ)
        column = vir_col[pl.ds(pl.multiple_of(part * pairs, pairs), pairs), :]
        energies = vir_ref[pl.ds(part * lane_tiles, lane_tiles), :]
        vec = trials[s].T
        col_r, col_l = [
            jnp.concatenate(
                [
                    jnp.broadcast_to(vec[:, k : k + 1], (LANES, LANES))
                    for k in range(first, first + lane_tiles)
                ],
                0,
            )
            for first in (0, lane_tiles)
        ]
        for t in range(lane_tiles):
            lanes = slice(t * LANES, (t + 1) * LANES)
            inverse = pl.reciprocal((shift - energies[t : t + 1, :]) - column, approx=True)
            w_right[:, lanes] = (inverse * col_r).astype(BF16)
            w_left[:, lanes] = (inverse * col_l).astype(BF16)
        b = jnp.concatenate(
            [lane_tile(b_straight, b_crossed, s, t) for t in range(lane_tiles)], 1
        )
        x_r = jnp.concatenate(
            [lane_tile(r_straight, r_crossed, s, t) for t in range(lane_tiles)], 1
        )
        x_l = jnp.concatenate(
            [lane_tile(l_straight, l_crossed, s, t) for t in range(lane_tiles)], 1
        )
        both = jnp.dot(
            jnp.concatenate([x_r, b], 0), w_right[...], preferred_element_type=F32
        )
        t_r, t_b = both[:slab_rows], both[slab_rows:]
        t_l = jnp.dot(x_l, w_left[...], preferred_element_type=F32)
        y_r = jnp.concatenate([y_ref[0]] * lane_tiles, 1)
        y_l = jnp.concatenate([y_ref[1]] * lane_tiles, 1)
        b = b.astype(F32)
        sig_r = jnp.sum(b * (t_r + y_r) + x_r.astype(F32) * t_b, 0, keepdims=True)
        sig_l = jnp.sum(b * (t_l + y_l), 0, keepdims=True)
        for t in range(lane_tiles):
            lanes = slice(t * LANES, (t + 1) * LANES)
            share[s, t : t + 1, :] = sig_r[:, lanes]
            share[s, lane_tiles + t : lane_tiles + t + 1, :] = sig_l[:, lanes]

        @pl.when(step < n - 1)
        def _():
            share_copy(s, me).start()

        return carry

    lax.fori_loop(0, n, slab_step, 0)

    own = lax.rem(me, per_occ)
    energies = vir_ref[pl.ds(own * lane_tiles, lane_tiles), :] - occ_ref[me // per_occ]
    total = jnp.concatenate([energies, energies], 0) * trial_ref[...] + share[me]

    def collect(step, total):
        source = peer(step)
        share_copy(source, source).wait_recv()
        return total + arrived[source]

    out_ref[...] = lax.fori_loop(0, n - 1, collect, total)

    def wait_sent(step, carry):
        gather_copy(peer(step), me).wait_send()
        share_copy(peer(step), me).wait_send()
        return carry

    lax.fori_loop(0, n - 1, wait_sent, 0)


def on_device(
    blocks,
    right_xform,
    left_xform,
    owner,
    tile_slot,
    domain,
    live_count,
    right_vec,
    left_vec,
    occ_energy,
    vir_energy,
    omega,
):
    n = lax.axis_size("aux")
    nb_local, flat_width = blocks.shape
    pairs = right_vec.shape[0]
    lane_tiles = pairs // LANES
    tiles = 2 * lane_tiles
    is_live = jnp.arange(nb_local, dtype=jnp.int32) < live_count[0]
    code = jnp.where(is_live, (owner[:, 0] * ADOM_DEV + domain) * tiles + tile_slot, -1)
    slots = jnp.arange(n * ADOM_DEV * tiles, dtype=jnp.int32)
    block_of = jnp.min(
        jnp.where(
            code[None, :] == slots[:, None], jnp.arange(nb_local, dtype=jnp.int32)[None, :], nb_local
        ),
        axis=1,
    )
    trial = jnp.concatenate([right_vec, left_vec]).reshape(2 * lane_tiles, LANES)
    vir = vir_energy.reshape(NVIR // LANES, LANES)
    sub = flat_width // LANES
    vmem, smem = (
        pl.BlockSpec(memory_space=pltpu.VMEM),
        pl.BlockSpec(memory_space=pltpu.SMEM),
    )
    out = pl.pallas_call(
        functools.partial(kernel, n),
        out_shape=jax.ShapeDtypeStruct((2 * lane_tiles, LANES), F32),
        in_specs=[smem] * 3 + [vmem] * 7,
        out_specs=vmem,
        scratch_shapes=[
            pltpu.VMEM((nb_local * (sub + 8), LANES), F32),
            *[pltpu.VMEM((nb_local + 1, sub, LANES), BF16)] * 6,
            pltpu.VMEM((NVIR, LANES), F32),
            pltpu.VMEM((pairs, pairs), BF16),
            pltpu.VMEM((pairs, pairs), BF16),
            pltpu.VMEM((2, ADOM_DEV * BLK, LANES), F32),
            pltpu.VMEM((n, 2 * lane_tiles, LANES), F32),
            pltpu.VMEM((n, 2 * lane_tiles, LANES), F32),
            pltpu.VMEM((n, 2 * lane_tiles, LANES), F32),
            pltpu.SemaphoreType.DMA((n,)),
            pltpu.SemaphoreType.DMA((n,)),
            pltpu.SemaphoreType.DMA((n,)),
            pltpu.SemaphoreType.DMA((n,)),
        ],
        compiler_params=pltpu.CompilerParams(
            collective_id=0, has_side_effects=True, vmem_limit_bytes=56 * 1024 * 1024
        ),
    )(occ_energy, omega, block_of, code[None, :], code[:, None], blocks, right_xform, left_xform, trial, vir)
    return out[:lane_tiles].reshape(pairs), out[lane_tiles:].reshape(pairs)


def solution(mesh):
    in_specs = (
        P(("groups", "aux"), None),
        P(("groups", "aux"), None),
        P(("groups", "aux"), None),
        P(("groups", "aux"), None),
        P(("groups", "aux")),
        P(("groups", "aux")),
        P(("groups", "aux")),
        P(("groups", "aux")),
        P(("groups", "aux")),
        P("groups"),
        P("groups"),
        P("groups"),
    )
    out_specs = (P(("groups", "aux")), P(("groups", "aux")))
    return jax.shard_map(
        on_device, mesh=mesh, in_specs=in_specs, out_specs=out_specs, check_vma=False
    )
```

time: 54.9 us -> 43.7 us (0.80)
  Pallas kernels: 49.4 us -> 37.4 us
  local copies, waits for them, and re-layouts: 2.11 us -> 2.74 us
    pallas_call x1, Pallas kernels: 49.4 us -> 37.4 us  [on_device(): pl.pallas_call(functools.partial(kernel, n), out_shape=jax.ShapeDtypeStru...]
    broadcast_in_dim x0 -> x1, local copies, waits for them, and re-layouts: none -> 0.73 us  [on_device(): code[:, None]]
    reduce_min x0 -> x1, other arithmetic: none -> 0.73 us  [on_device(): jnp.min(jnp.where(code[None, :] == slots[:, None], jnp.arange(nb_local, d...]
    concatenate x1 -> x0, other arithmetic: 0.57 us -> none  [on_device(): jnp.concatenate([jnp.where(is_live & (tile_slot % 2 == half), slot, -1) f...]
where the time goes in v2:
time: 43.7 us; the launch traced here: 43.5 us
  Pallas kernels  37.4 us (86%)
  local copies, waits for them, and re-layouts  2.74 us (6%)
  between operations  1.98 us (5%)
  other arithmetic  1.34 us (3%)
    pallas_call x1, Pallas kernels, on_device(): pl.pallas_call(functools.partial(kernel, n), out_shape=jax.ShapeDtypeStru...  37.4 us
    reshape x1, local copies, waits for them, and re-layouts, on_device(): return (out[:lane_tiles].reshape(pairs), out[lane_tiles:].reshape(pairs))  1.33 us

profile of v2, /device:TPU:1, one launch (start us, length us, event | category | flops | bytes accessed | tf_op | source)
XLA Modules:
  0.0 43.5 jit_solution(1771130467654319261)
XLA Ops:
  1.9 0.0 copy-start.3
  1.9 0.0 copy-start.4
  1.9 0.0 copy-start.5
  2.0 0.6 %copy-done.3 = s32[128]{0:T(128)S(1)} copy-done((s32[128]{0:T(128)S(1)}, s32[128]{0:T(128)}, u32[]{:S(2)}) %copy-start.3) | copy-done | bytes 536
  2.6 0.0 copy-done.4
  2.6 0.0 copy-done.5
  2.6 0.0 copy-start
  2.6 0.0 copy-start.1
  2.6 0.0 copy-start.2
  2.6 0.7 %select_reduce_fusion.block_of_ref = s32[384]{0:T(512)} fusion(s32[128]{0:T(128)S(1)} %compare_select_fusion), kind=kLoop, calls=%fused_computation | loop fusion | flops 147072 | bytes 2048 | tf_op jit(solution)/shard_map/reduce_min | solution.py:261
  3.4 0.0 copy-done.1
  3.4 0.0 copy-done.2
  3.4 0.6 %pad_maximum_fusion.trial_ref = f32[8,128]{1,0:T(8,128)} fusion(f32[4,128]{1,0:T(4,128)S(1)} %bitcast.22, f32[4,128]{1,0:T(4,128)S(1)} %bitcast.23), kind=kLoop, calls=%fused_computation.2 | loop fusion | flops 1024 | bytes 8192 | tf_op jit(solution)/shard_map/concatenate | solution.py:267
  4.0 0.0 copy-done
  4.0 0.7 %copy.15.code_col_ref = s32[128,1]{1,0:T(8,128)} copy(s32[128,1]{0,1:T(1,128)S(1)} %bitcast.20) | data formatting | bytes 1024 | tf_op jit(solution)/shard_map/broadcast_in_dim | solution.py:297
  4.7 37.4 %shard_map.131 = f32[8,128]{1,0:T(8,128)} custom-call(f32[4]{0:T(128)} %occ_ref.1, f32[1]{0:T(128)S(6)} %copy.17.omega_ref, s32[384]{0:T(512)} %select_reduce_fusion.block_of_ref, s32[1,128]{1,0:T(1,128)} %bitcast.21, s32[128,1]{1,0:T(8,128)} %copy.15.code_col_ref, bf16[128,4096]{1,0:T(8,128)(2,1)} %blocks_ref.1, bf16[128,4096]{1,0:T(8,128)(2,1)} %right_ref.1, ...), custom_call_target="tpu_custom_call" | custom-call | tf_op jit(solution)/shard_map/pallas_call | solution.py:274
  42.2 1.3 %slice_bitcast_fusion = (f32[512]{0:T(512)}, f32[512]{0:T(512)}) fusion(f32[8,128]{1,0:T(8,128)} %shard_map.131), kind=kLoop, calls=%fused_computation.3 | loop fusion | bytes 8192 | tf_op jit(solution)/shard_map/reshape | solution.py:298
  (1 shorter events, 0.0 us)
Async XLA Ops:
  1.9 0.7 %copy-start.3 = (s32[128]{0:T(128)S(1)}, s32[128]{0:T(128)}, u32[]{:S(2)}) copy-start(s32[128]{0:T(128)} %param.16) | copy-start | bytes 1540
  1.9 0.7 %copy-start.4 = (s32[128]{0:T(128)S(1)}, s32[128]{0:T(128)}, u32[]{:S(2)}) copy-start(s32[128]{0:T(128)} %param.17) | copy-start | bytes 1540
  1.9 0.7 %copy-start.5 = (s32[128,1]{0,1:T(1,128)S(1)}, s32[128,1]{0,1:T(1,128)}, u32[]{:S(2)}) copy-start(s32[128,1]{0,1:T(1,128)} %param.15) | copy-start | bytes 1540
  2.6 1.4 %copy-start = (s32[128]{0:T(128)}, s32[128]{0:T(128)S(1)}, u32[]{:S(2)}) copy-start(s32[128]{0:T(128)S(1)} %compare_select_fusion) | copy-start | bytes 1540
  2.6 0.8 %copy-start.1 = (f32[512]{0:T(512)S(1)}, f32[512]{0:T(512)}, u32[]{:S(2)}) copy-start(f32[512]{0:T(512)} %param.20) | copy-start | bytes 6148
  2.6 0.7 %copy-start.2 = (f32[512]{0:T(512)S(1)}, f32[512]{0:T(512)}, u32[]{:S(2)}) copy-start(f32[512]{0:T(512)} %param.19) | copy-start | bytes 6148

commit v3 on v2

--- a/solution.py
+++ b/solution.py
@@ -11,6 +11,7 @@
 NVIR = 2048
 ADOM_DEV = 3
 LANES = 128
+WIDE = 8
 F32 = jnp.float32
 BF16 = jnp.bfloat16
 
@@ -28,7 +29,9 @@
     trial_ref,
     vir_ref,
     out_ref,
-    turned,
+    turned_b,
+    turned_r,
+    turned_l,
     b_straight,
     b_crossed,
     r_straight,
@@ -36,8 +39,10 @@
     l_straight,
     l_crossed,
     vir_col,
-    w_right,
-    w_left,
+    w_right0,
+    w_left0,
+    w_right1,
+    w_left1,
     y_ref,
     trials,
     share,
@@ -48,13 +53,13 @@
     share_recv,
 ):
     me = lax.axis_index("aux")
-    pairs = w_right.shape[0]
+    pairs = w_right0.shape[0]
     lane_tiles = pairs // LANES
     tiles = 2 * lane_tiles
     sub = BLK * BLK // LANES
     slab_rows = ADOM_DEV * BLK
     nb = blocks_ref.shape[0]
-    pitch = turned.shape[0] // nb
+    pitch = turned_b.shape[0] // nb
 
     def peer(step):
         return lax.rem(me + 1 + step, n)
@@ -100,29 +105,37 @@
 
     same = jnp.where(code_col_ref[...] == code_row_ref[...], 1.0, 0.0).astype(BF16)
 
-    def assemble(source_ref, straight, crossed):
-        def chunk(j, carry):
-            first = pl.multiple_of(j * 2 * LANES, 2 * LANES)
+    arrays = (
+        (blocks_ref, turned_b, b_straight, b_crossed),
+        (right_ref, turned_r, r_straight, r_crossed),
+        (left_ref, turned_l, l_straight, l_crossed),
+    )
+
+    def merge(j, carry):
+        first = pl.multiple_of(j * WIDE * LANES, WIDE * LANES)
+        for source_ref, turned, _, _ in arrays:
             merged = jnp.dot(
-                same, source_ref[:, pl.ds(first, 2 * LANES)], preferred_element_type=F32
+                same, source_ref[:, pl.ds(first, WIDE * LANES)], preferred_element_type=F32
             )
-            for half in range(2):
-                turned[pl.ds(j * 2 + half, nb, stride=pitch), :] = merged[
-                    :, half * LANES : (half + 1) * LANES
+            for k in range(WIDE):
+                turned[pl.ds(j * WIDE + k, nb, stride=pitch), :] = merged[
+                    :, k * LANES : (k + 1) * LANES
                 ]
-            return carry
-
-        lax.fori_loop(0, sub // 2, chunk, 0)
-
-        def settle(i, carry):
-            for k in range(8):
-                b = i * 8 + k
+        return carry
+
+    lax.fori_loop(0, sub // WIDE, merge, 0)
+
+    def settle(i, carry):
+        for _, turned, straight, crossed in arrays:
+            for k in range(4):
+                b = i * 4 + k
                 x = turned[pl.ds(pl.multiple_of(b * pitch, 8), sub), :]
                 straight[b] = x.astype(BF16)
                 crossed[b] = pltpu.roll(x, BLK, 1).astype(BF16)
-            return carry
-
-        lax.fori_loop(0, nb // 8, settle, 0)
+        return carry
+
+    lax.fori_loop(0, nb // 4, settle, 0)
+    for _, _, straight, crossed in arrays:
         straight[nb] = jnp.zeros((sub, LANES), BF16)
         crossed[nb] = jnp.zeros((sub, LANES), BF16)
 
@@ -137,10 +150,6 @@
             parts.append(jnp.where(low, crossed[first], straight[second]))
         return jnp.concatenate(parts, 0)
 
-    assemble(blocks_ref, b_straight, b_crossed)
-    assemble(right_ref, r_straight, r_crossed)
-    assemble(left_ref, l_straight, l_crossed)
-
     def wait_gather(step, carry):
         gather_copy(peer(step), peer(step)).wait_recv()
         return carry
@@ -163,8 +172,7 @@
 
     per_occ = NVIR // pairs
 
-    def slab_step(step, carry):
-        s = peer(step)
+    def weights(s, w_right, w_left):
         shift = omega_ref[0] + 2.0 * occ_ref[s // per_occ]
         part = lax.rem(s, per_occ)
         column = vir_col[pl.ds(pl.multiple_of(part * pairs, pairs), pairs), :]
@@ -185,15 +193,12 @@
             inverse = pl.reciprocal((shift - energies[t : t + 1, :]) - column, approx=True)
             w_right[:, lanes] = (inverse * col_r).astype(BF16)
             w_left[:, lanes] = (inverse * col_l).astype(BF16)
-        b = jnp.concatenate(
-            [lane_tile(b_straight, b_crossed, s, t) for t in range(lane_tiles)], 1
-        )
-        x_r = jnp.concatenate(
-            [lane_tile(r_straight, r_crossed, s, t) for t in range(lane_tiles)], 1
-        )
-        x_l = jnp.concatenate(
-            [lane_tile(l_straight, l_crossed, s, t) for t in range(lane_tiles)], 1
-        )
+
+    def slab_term(s, w_right, w_left):
+        b, x_r, x_l = [
+            jnp.concatenate([lane_tile(straight, crossed, s, t) for t in range(lane_tiles)], 1)
+            for _, _, straight, crossed in arrays
+        ]
         both = jnp.dot(
             jnp.concatenate([x_r, b], 0), w_right[...], preferred_element_type=F32
         )
@@ -209,13 +214,22 @@
             share[s, t : t + 1, :] = sig_r[:, lanes]
             share[s, lane_tiles + t : lane_tiles + t + 1, :] = sig_l[:, lanes]
 
-        @pl.when(step < n - 1)
+    weights(peer(0), w_right0, w_left0)
+
+    def two_slabs(i, carry):
+        weights(peer(2 * i + 1), w_right1, w_left1)
+        slab_term(peer(2 * i), w_right0, w_left0)
+        weights(peer(2 * i + 2), w_right0, w_left0)
+        slab_term(peer(2 * i + 1), w_right1, w_left1)
+        share_copy(peer(2 * i), me).start()
+
+        @pl.when(2 * i + 1 < n - 1)
         def _():
-            share_copy(s, me).start()
-
-        return carry
-
-    lax.fori_loop(0, n, slab_step, 0)
+            share_copy(peer(2 * i + 1), me).start()
+
+        return carry
+
+    lax.fori_loop(0, n // 2, two_slabs, 0)
 
     own = lax.rem(me, per_occ)
     energies = vir_ref[pl.ds(own * lane_tiles, lane_tiles), :] - occ_ref[me // per_occ]
@@ -277,11 +291,10 @@
         in_specs=[smem] * 3 + [vmem] * 7,
         out_specs=vmem,
         scratch_shapes=[
-            pltpu.VMEM((nb_local * (sub + 8), LANES), F32),
+            *[pltpu.VMEM((nb_local * (sub + 8), LANES), F32)] * 3,
             *[pltpu.VMEM((nb_local + 1, sub, LANES), BF16)] * 6,
             pltpu.VMEM((NVIR, LANES), F32),
-            pltpu.VMEM((pairs, pairs), BF16),
-            pltpu.VMEM((pairs, pairs), BF16),
+            *[pltpu.VMEM((pairs, pairs), BF16)] * 4,
             pltpu.VMEM((2, ADOM_DEV * BLK, LANES), F32),
             pltpu.VMEM((n, 2 * lane_tiles, LANES), F32),
             pltpu.VMEM((n, 2 * lane_tiles, LANES), F32),

time: 43.7 us -> 35.3 us (0.81)
  Pallas kernels: 37.4 us -> 29.1 us
    pallas_call x1, Pallas kernels: 37.4 us -> 29.1 us  [on_device(): pl.pallas_call(functools.partial(kernel, n), out_shape=jax.ShapeDtypeStru...]
where the time goes in v3:
time: 35.3 us; the launch traced here: 35.1 us
  Pallas kernels  29.1 us (82%)
  local copies, waits for them, and re-layouts  2.74 us (8%)
  between operations  1.98 us (6%)
  other arithmetic  1.34 us (4%)
    pallas_call x1, Pallas kernels, on_device(): pl.pallas_call(functools.partial(kernel, n), out_shape=jax.ShapeDtypeStru...  29.1 us
    reshape x1, local copies, waits for them, and re-layouts, on_device(): return (out[:lane_tiles].reshape(pairs), out[lane_tiles:].reshape(pairs))  1.33 us
    broadcast_in_dim x1, local copies, waits for them, and re-layouts, on_device(): code[:, None]  0.73 us
    reduce_min x1, other arithmetic, on_device(): jnp.min(jnp.where(code[None, :] == slots[:, None], jnp.arange(nb_local, d...  0.73 us

profile of v3, /device:TPU:1, one launch (start us, length us, event | category | flops | bytes accessed | tf_op | source)
XLA Modules:
  0.0 35.1 jit_solution(8578075071780967366)
XLA Ops:
  1.9 0.0 copy-start.3
  1.9 0.0 copy-start.4
  1.9 0.0 copy-start.5
  2.0 0.6 %copy-done.3 = s32[128]{0:T(128)S(1)} copy-done((s32[128]{0:T(128)S(1)}, s32[128]{0:T(128)}, u32[]{:S(2)}) %copy-start.3) | copy-done | bytes 536
  2.6 0.0 copy-done.4
  2.6 0.0 copy-done.5
  2.6 0.0 copy-start
  2.6 0.0 copy-start.1
  2.6 0.0 copy-start.2
  2.6 0.7 %select_reduce_fusion.block_of_ref = s32[384]{0:T(512)} fusion(s32[128]{0:T(128)S(1)} %compare_select_fusion), kind=kLoop, calls=%fused_computation | loop fusion | flops 147072 | bytes 2048 | tf_op jit(solution)/shard_map/reduce_min | solution.py:275
  3.4 0.0 copy-done.1
  3.4 0.0 copy-done.2
  3.4 0.6 %pad_maximum_fusion.trial_ref = f32[8,128]{1,0:T(8,128)} fusion(f32[4,128]{1,0:T(4,128)S(1)} %bitcast.22, f32[4,128]{1,0:T(4,128)S(1)} %bitcast.23), kind=kLoop, calls=%fused_computation.2 | loop fusion | flops 1024 | bytes 8192 | tf_op jit(solution)/shard_map/concatenate | solution.py:281
  4.0 0.0 copy-done
  4.0 0.7 %copy.15.code_col_ref = s32[128,1]{1,0:T(8,128)} copy(s32[128,1]{0,1:T(1,128)S(1)} %bitcast.20) | data formatting | bytes 1024 | tf_op jit(solution)/shard_map/broadcast_in_dim | solution.py:310
  4.7 29.1 %shard_map.131 = f32[8,128]{1,0:T(8,128)} custom-call(f32[4]{0:T(128)} %occ_ref.1, f32[1]{0:T(128)S(6)} %copy.17.omega_ref, s32[384]{0:T(512)} %select_reduce_fusion.block_of_ref, s32[1,128]{1,0:T(1,128)} %bitcast.21, s32[128,1]{1,0:T(8,128)} %copy.15.code_col_ref, bf16[128,4096]{1,0:T(8,128)(2,1)} %blocks_ref.1, bf16[128,4096]{1,0:T(8,128)(2,1)} %right_ref.1, ...), custom_call_target="tpu_custom_call" | custom-call | tf_op jit(solution)/shard_map/pallas_call | solution.py:288
  33.8 1.3 %slice_bitcast_fusion = (f32[512]{0:T(512)}, f32[512]{0:T(512)}) fusion(f32[8,128]{1,0:T(8,128)} %shard_map.131), kind=kLoop, calls=%fused_computation.3 | loop fusion | bytes 8192 | tf_op jit(solution)/shard_map/reshape | solution.py:311
  (1 shorter events, 0.0 us)
Async XLA Ops:
  1.9 0.7 %copy-start.3 = (s32[128]{0:T(128)S(1)}, s32[128]{0:T(128)}, u32[]{:S(2)}) copy-start(s32[128]{0:T(128)} %param.16) | copy-start | bytes 1540
  1.9 0.7 %copy-start.4 = (s32[128]{0:T(128)S(1)}, s32[128]{0:T(128)}, u32[]{:S(2)}) copy-start(s32[128]{0:T(128)} %param.17) | copy-start | bytes 1540
  1.9 0.7 %copy-start.5 = (s32[128,1]{0,1:T(1,128)S(1)}, s32[128,1]{0,1:T(1,128)}, u32[]{:S(2)}) copy-start(s32[128,1]{0,1:T(1,128)} %param.15) | copy-start | bytes 1540
  2.6 1.4 %copy-start = (s32[128]{0:T(128)}, s32[128]{0:T(128)S(1)}, u32[]{:S(2)}) copy-start(s32[128]{0:T(128)S(1)} %compare_select_fusion) | copy-start | bytes 1540
  2.6 0.8 %copy-start.1 = (f32[512]{0:T(512)S(1)}, f32[512]{0:T(512)}, u32[]{:S(2)}) copy-start(f32[512]{0:T(512)} %param.20) | copy-start | bytes 6148
  2.6 0.7 %copy-start.2 = (f32[512]{0:T(512)S(1)}, f32[512]{0:T(512)}, u32[]{:S(2)}) copy-start(f32[512]{0:T(512)} %param.19) | copy-start | bytes 6148

commit v4 on v3

--- a/solution.py
+++ b/solution.py
@@ -12,6 +12,7 @@
 ADOM_DEV = 3
 LANES = 128
 WIDE = 8
+PART = 2
 F32 = jnp.float32
 BF16 = jnp.bfloat16
 
@@ -20,15 +21,25 @@
     n,
     occ_ref,
     omega_ref,
-    block_of_ref,
-    code_row_ref,
-    code_col_ref,
+    live_ref,
+    owner_ref,
+    slot_ref,
+    domain_ref,
+    blocks_hbm,
+    right_hbm,
+    left_hbm,
+    right_vec_ref,
+    left_vec_ref,
+    vir_ref,
+    out_ref,
     blocks_ref,
     right_ref,
     left_ref,
+    load_sem,
+    table,
+    block_of_ref,
+    table_sem,
     trial_ref,
-    vir_ref,
-    out_ref,
     turned_b,
     turned_r,
     turned_l,
@@ -70,13 +81,42 @@
         pl.semaphore_signal(barrier, inc=1, device_id={"aux": peer(step)})
         return carry
 
+    loads = [
+        pltpu.make_async_copy(source, target, load_sem.at[k])
+        for k, (source, target) in enumerate(
+            ((blocks_hbm, blocks_ref), (right_hbm, right_ref), (left_hbm, left_ref))
+        )
+    ]
+    for load in loads:
+        load.start()
     lax.fori_loop(0, n - 1, greet, 0)
+
+    trial_ref[:lane_tiles, :] = right_vec_ref[...]
+    trial_ref[lane_tiles:, :] = left_vec_ref[...]
+    trials[me] = trial_ref[...]
+
+    live = lax.broadcasted_iota(jnp.int32, (1, nb), 1) < live_ref[...]
+    code = (owner_ref[...] * ADOM_DEV + domain_ref[...]) * tiles + slot_ref[...]
+    code = jnp.where(live, code, -1).astype(F32)
+    code_row = jnp.broadcast_to(code, (nb, nb))
+    code_col = code_row.T
+    same = jnp.where(code_col == code_row, 1.0, 0.0).astype(BF16)
+    block_ids = lax.broadcasted_iota(jnp.int32, (nb, LANES), 0)
+    lane_ids = lax.broadcasted_iota(jnp.int32, (nb, LANES), 1)
+
+    def fill(s, carry):
+        slots = (lane_ids + s * (ADOM_DEV * tiles)).astype(F32)
+        held = jnp.where(code_col[:, :LANES] == slots, block_ids, nb)
+        table[pl.ds(s, 1), :] = jnp.min(held, 0, keepdims=True)
+        return carry
+
+    lax.fori_loop(0, n, fill, 0)
+    to_scalars = pltpu.make_async_copy(table, block_of_ref, table_sem)
+    to_scalars.start()
 
     for i in range(NVIR // LANES):
         row = jnp.broadcast_to(vir_ref[i : i + 1, :], (LANES, LANES))
         vir_col[i * LANES : (i + 1) * LANES, :] = row.T
-
-    pl.semaphore_wait(barrier, n - 1)
 
     def gather_copy(target, source):
         return pltpu.make_async_remote_copy(
@@ -99,11 +139,6 @@
     def start_gather(step, carry):
         gather_copy(peer(step), me).start()
         return carry
-
-    lax.fori_loop(0, n - 1, start_gather, 0)
-    trials[me] = trial_ref[...]
-
-    same = jnp.where(code_col_ref[...] == code_row_ref[...], 1.0, 0.0).astype(BF16)
 
     arrays = (
         (blocks_ref, turned_b, b_straight, b_crossed),
@@ -123,15 +158,20 @@
                 ]
         return carry
 
+    for load in loads:
+        load.wait()
     lax.fori_loop(0, sub // WIDE, merge, 0)
+    pl.semaphore_wait(barrier, n - 1)
+    lax.fori_loop(0, n - 1, start_gather, 0)
 
     def settle(i, carry):
         for _, turned, straight, crossed in arrays:
             for k in range(4):
                 b = i * 4 + k
                 x = turned[pl.ds(pl.multiple_of(b * pitch, 8), sub), :]
-                straight[b] = x.astype(BF16)
-                crossed[b] = pltpu.roll(x, BLK, 1).astype(BF16)
+                x = x.astype(BF16)
+                straight[b] = x
+                crossed[b] = jnp.concatenate([x[:, BLK:], x[:, :BLK]], 1)
         return carry
 
     lax.fori_loop(0, nb // 4, settle, 0)
@@ -144,8 +184,8 @@
     def lane_tile(straight, crossed, s, t):
         parts = []
         for d in range(ADOM_DEV):
-            slot = s * (ADOM_DEV * tiles) + d * tiles + 2 * t
-            first, second = block_of_ref[slot], block_of_ref[slot + 1]
+            slot = d * tiles + 2 * t
+            first, second = block_of_ref[s, slot], block_of_ref[s, slot + 1]
             parts.append(jnp.where(low, straight[first], crossed[second]))
             parts.append(jnp.where(low, crossed[first], straight[second]))
         return jnp.concatenate(parts, 0)
@@ -155,6 +195,8 @@
         return carry
 
     lax.fori_loop(0, n - 1, wait_gather, 0)
+
+    to_scalars.wait()
 
     def add_y(s, state):
         acc_r, acc_l = state
@@ -172,13 +214,9 @@
 
     per_occ = NVIR // pairs
 
-    def weights(s, w_right, w_left):
-        shift = omega_ref[0] + 2.0 * occ_ref[s // per_occ]
-        part = lax.rem(s, per_occ)
-        column = vir_col[pl.ds(pl.multiple_of(part * pairs, pairs), pairs), :]
-        energies = vir_ref[pl.ds(part * lane_tiles, lane_tiles), :]
+    def columns(s):
         vec = trials[s].T
-        col_r, col_l = [
+        return [
             jnp.concatenate(
                 [
                     jnp.broadcast_to(vec[:, k : k + 1], (LANES, LANES))
@@ -188,44 +226,55 @@
             )
             for first in (0, lane_tiles)
         ]
-        for t in range(lane_tiles):
+
+    def weights(s, cols, w_right, w_left, lane_tile_ids):
+        shift = omega_ref[...] + 2.0 * occ_ref[s // per_occ]
+        part = lax.rem(s, per_occ)
+        column = vir_col[pl.ds(pl.multiple_of(part * pairs, pairs), pairs), :]
+        energies = vir_ref[pl.ds(part * lane_tiles, lane_tiles), :]
+        for t in lane_tile_ids:
             lanes = slice(t * LANES, (t + 1) * LANES)
             inverse = pl.reciprocal((shift - energies[t : t + 1, :]) - column, approx=True)
-            w_right[:, lanes] = (inverse * col_r).astype(BF16)
-            w_left[:, lanes] = (inverse * col_l).astype(BF16)
-
-    def slab_term(s, w_right, w_left):
+            w_right[:, lanes] = (inverse * cols[0]).astype(BF16)
+            w_left[:, lanes] = (inverse * cols[1]).astype(BF16)
+
+    def slab_term(s, w_right, w_left, later, later_right, later_left):
         b, x_r, x_l = [
             jnp.concatenate([lane_tile(straight, crossed, s, t) for t in range(lane_tiles)], 1)
             for _, _, straight, crossed in arrays
         ]
-        both = jnp.dot(
-            jnp.concatenate([x_r, b], 0), w_right[...], preferred_element_type=F32
-        )
-        t_r, t_b = both[:slab_rows], both[slab_rows:]
-        t_l = jnp.dot(x_l, w_left[...], preferred_element_type=F32)
-        y_r = jnp.concatenate([y_ref[0]] * lane_tiles, 1)
-        y_l = jnp.concatenate([y_ref[1]] * lane_tiles, 1)
-        b = b.astype(F32)
-        sig_r = jnp.sum(b * (t_r + y_r) + x_r.astype(F32) * t_b, 0, keepdims=True)
-        sig_l = jnp.sum(b * (t_l + y_l), 0, keepdims=True)
-        for t in range(lane_tiles):
-            lanes = slice(t * LANES, (t + 1) * LANES)
-            share[s, t : t + 1, :] = sig_r[:, lanes]
-            share[s, lane_tiles + t : lane_tiles + t + 1, :] = sig_l[:, lanes]
-
-    weights(peer(0), w_right0, w_left0)
+        stacked = jnp.concatenate([x_r, b], 0)
+        cols = columns(later)
+        for first in range(0, lane_tiles, PART):
+            part = range(first, first + PART)
+            lanes = slice(first * LANES, (first + PART) * LANES)
+            weights(later, cols, later_right, later_left, part)
+            both = jnp.dot(stacked, w_right[:, lanes], preferred_element_type=F32)
+            t_r, t_b = both[:slab_rows], both[slab_rows:]
+            t_l = jnp.dot(x_l, w_left[:, lanes], preferred_element_type=F32)
+            y_r = jnp.concatenate([y_ref[0]] * PART, 1)
+            y_l = jnp.concatenate([y_ref[1]] * PART, 1)
+            b_part = b[:, lanes].astype(F32)
+            sig_r = jnp.sum(
+                b_part * (t_r + y_r) + x_r[:, lanes].astype(F32) * t_b, 0, keepdims=True
+            )
+            sig_l = jnp.sum(b_part * (t_l + y_l), 0, keepdims=True)
+            for k, t in enumerate(part):
+                lanes = slice(k * LANES, (k + 1) * LANES)
+                share[s, t : t + 1, :] = sig_r[:, lanes]
+                share[s, lane_tiles + t : lane_tiles + t + 1, :] = sig_l[:, lanes]
+
+    weights(peer(0), columns(peer(0)), w_right0, w_left0, range(lane_tiles))
 
     def two_slabs(i, carry):
-        weights(peer(2 * i + 1), w_right1, w_left1)
-        slab_term(peer(2 * i), w_right0, w_left0)
-        weights(peer(2 * i + 2), w_right0, w_left0)
-        slab_term(peer(2 * i + 1), w_right1, w_left1)
-        share_copy(peer(2 * i), me).start()
+        now, then, after = peer(2 * i), peer(2 * i + 1), peer(2 * i + 2)
+        slab_term(now, w_right0, w_left0, then, w_right1, w_left1)
+        share_copy(now, me).start()
+        slab_term(then, w_right1, w_left1, after, w_right0, w_left0)
 
         @pl.when(2 * i + 1 < n - 1)
         def _():
-            share_copy(peer(2 * i + 1), me).start()
+            share_copy(then, me).start()
 
         return carry
 
@@ -268,17 +317,6 @@
     nb_local, flat_width = blocks.shape
     pairs = right_vec.shape[0]
     lane_tiles = pairs // LANES
-    tiles = 2 * lane_tiles
-    is_live = jnp.arange(nb_local, dtype=jnp.int32) < live_count[0]
-    code = jnp.where(is_live, (owner[:, 0] * ADOM_DEV + domain) * tiles + tile_slot, -1)
-    slots = jnp.arange(n * ADOM_DEV * tiles, dtype=jnp.int32)
-    block_of = jnp.min(
-        jnp.where(
-            code[None, :] == slots[:, None], jnp.arange(nb_local, dtype=jnp.int32)[None, :], nb_local
-        ),
-        axis=1,
-    )
-    trial = jnp.concatenate([right_vec, left_vec]).reshape(2 * lane_tiles, LANES)
     vir = vir_energy.reshape(NVIR // LANES, LANES)
     sub = flat_width // LANES
     vmem, smem = (
@@ -288,9 +326,15 @@
     out = pl.pallas_call(
         functools.partial(kernel, n),
         out_shape=jax.ShapeDtypeStruct((2 * lane_tiles, LANES), F32),
-        in_specs=[smem] * 3 + [vmem] * 7,
+        in_specs=[smem] + [vmem] * 5 + [pl.BlockSpec(memory_space=pl.ANY)] * 3 + [vmem] * 3,
         out_specs=vmem,
         scratch_shapes=[
+            *[pltpu.VMEM(blocks.shape, BF16)] * 3,
+            pltpu.SemaphoreType.DMA((3,)),
+            pltpu.VMEM((n, LANES), jnp.int32),
+            pltpu.SMEM((n, LANES), jnp.int32),
+            pltpu.SemaphoreType.DMA(()),
+            pltpu.VMEM((2 * lane_tiles, LANES), F32),
             *[pltpu.VMEM((nb_local * (sub + 8), LANES), F32)] * 3,
             *[pltpu.VMEM((nb_local + 1, sub, LANES), BF16)] * 6,
             pltpu.VMEM((NVIR, LANES), F32),
@@ -307,7 +351,20 @@
         compiler_params=pltpu.CompilerParams(
             collective_id=0, has_side_effects=True, vmem_limit_bytes=56 * 1024 * 1024
         ),
-    )(occ_energy, omega, block_of, code[None, :], code[:, None], blocks, right_xform, left_xform, trial, vir)
+    )(
+        occ_energy,
+        omega.reshape(1, 1),
+        live_count.reshape(1, 1),
+        owner.reshape(1, nb_local),
+        tile_slot.reshape(1, nb_local),
+        domain.reshape(1, nb_local),
+        blocks,
+        right_xform,
+        left_xform,
+        right_vec.reshape(lane_tiles, LANES),
+        left_vec.reshape(lane_tiles, LANES),
+        vir,
+    )
     return out[:lane_tiles].reshape(pairs), out[lane_tiles:].reshape(pairs)
 
 

time: 35.3 us -> 31.3 us (0.89)
  local copies, waits for them, and re-layouts: 2.74 us -> 1.33 us
  other arithmetic: 1.34 us -> 0 us
  Pallas kernels: 29.1 us -> 27.8 us
    pallas_call x1, Pallas kernels: 29.1 us -> 27.8 us  [on_device(): pl.pallas_call(functools.partial(kernel, n), out_shape=jax.ShapeDtypeStru...]
    broadcast_in_dim x1 -> x0, local copies, waits for them, and re-layouts: 0.73 us -> none  [on_device(): code[:, None]]
    reduce_min x1 -> x0, other arithmetic: 0.73 us -> none  [on_device(): jnp.min(jnp.where(code[None, :] == slots[:, None], jnp.arange(nb_local, d...]
    unnamed x12 -> x0, local copies, waits for them, and re-layouts: 0.68 us -> none
    concatenate x1 -> x0, other arithmetic: 0.6 us -> none  [on_device(): jnp.concatenate([right_vec, left_vec]).reshape(2 * lane_tiles, LANES)]
where the time goes in v4:
time: 31.3 us; the launch traced here: 31.1 us
  Pallas kernels  27.8 us (89%)
  between operations  1.93 us (6%)
  local copies, waits for them, and re-layouts  1.33 us (4%)
    pallas_call x1, Pallas kernels, on_device(): pl.pallas_call(functools.partial(kernel, n), out_shape=jax.ShapeDtypeStru...  27.8 us
    reshape x1, local copies, waits for them, and re-layouts, on_device(): return (out[:lane_tiles].reshape(pairs), out[lane_tiles:].reshape(pairs))  1.33 us

profile of v4, /device:TPU:1, one launch (start us, length us, event | category | flops | bytes accessed | tf_op | source)
XLA Modules:
  0.0 31.1 jit_solution(4219778668962849161)
XLA Ops:
  1.9 27.8 %shard_map.131 = f32[8,128]{1,0:T(8,128)} custom-call(f32[4]{0:T(128)} %occ_ref.1, f32[1,1]{1,0:T(1,128)} %bitcast.13.omega_ref, s32[1,1]{1,0:T(1,128)} %bitcast.12.live_ref, s32[1,128]{1,0:T(1,128)} %bitcast.17, s32[1,128]{1,0:T(1,128)} %bitcast.18, s32[1,128]{1,0:T(1,128)} %bitcast.19, bf16[128,4096]{1,0:T(8,128)(2,1)} %blocks_hbm.1, ...), custom_call_target="tpu_custom_call" | custom-call | tf_op jit(solution)/shard_map/pallas_call | solution.py:326
  29.7 1.3 %slice_bitcast_fusion = (f32[512]{0:T(512)}, f32[512]{0:T(512)}) fusion(f32[8,128]{1,0:T(8,128)} %shard_map.131), kind=kLoop, calls=%fused_computation | loop fusion | bytes 8192 | tf_op jit(solution)/shard_map/reshape | solution.py:368

commit v5 on v4

--- a/solution.py
+++ b/solution.py
@@ -166,15 +166,15 @@
 
     def settle(i, carry):
         for _, turned, straight, crossed in arrays:
-            for k in range(4):
-                b = i * 4 + k
+            for k in range(16):
+                b = i * 16 + k
                 x = turned[pl.ds(pl.multiple_of(b * pitch, 8), sub), :]
                 x = x.astype(BF16)
                 straight[b] = x
                 crossed[b] = jnp.concatenate([x[:, BLK:], x[:, :BLK]], 1)
         return carry
 
-    lax.fori_loop(0, nb // 4, settle, 0)
+    lax.fori_loop(0, nb // 16, settle, 0)
     for _, _, straight, crossed in arrays:
         straight[nb] = jnp.zeros((sub, LANES), BF16)
         crossed[nb] = jnp.zeros((sub, LANES), BF16)

time: 31.3 us -> 31.3 us (level)
  no operation moved by 1% of the time
where the time goes in v5:
time: 31.3 us; the launch traced here: 31.1 us
  Pallas kernels  27.8 us (89%)
  between operations  1.93 us (6%)
  local copies, waits for them, and re-layouts  1.33 us (4%)
    pallas_call x1, Pallas kernels, on_device(): pl.pallas_call(functools.partial(kernel, n), out_shape=jax.ShapeDtypeStru...  27.8 us
    reshape x1, local copies, waits for them, and re-layouts, on_device(): return (out[:lane_tiles].reshape(pairs), out[lane_tiles:].reshape(pairs))  1.33 us

profile of v5, /device:TPU:1, one launch (start us, length us, event | category | flops | bytes accessed | tf_op | source)
XLA Modules:
  0.0 31.1 jit_solution(8823594916694679478)
XLA Ops:
  1.9 27.8 %shard_map.131 = f32[8,128]{1,0:T(8,128)} custom-call(f32[4]{0:T(128)} %occ_ref.1, f32[1,1]{1,0:T(1,128)} %bitcast.13.omega_ref, s32[1,1]{1,0:T(1,128)} %bitcast.12.live_ref, s32[1,128]{1,0:T(1,128)} %bitcast.17, s32[1,128]{1,0:T(1,128)} %bitcast.18, s32[1,128]{1,0:T(1,128)} %bitcast.19, bf16[128,4096]{1,0:T(8,128)(2,1)} %blocks_hbm.1, ...), custom_call_target="tpu_custom_call" | custom-call | tf_op jit(solution)/shard_map/pallas_call | solution.py:326
  29.7 1.3 %slice_bitcast_fusion = (f32[512]{0:T(512)}, f32[512]{0:T(512)}) fusion(f32[8,128]{1,0:T(8,128)} %shard_map.131), kind=kLoop, calls=%fused_computation | loop fusion | bytes 8192 | tf_op jit(solution)/shard_map/reshape | solution.py:368

commit v6 on v5

--- a/solution.py
+++ b/solution.py
@@ -158,11 +158,11 @@
                 ]
         return carry
 
+    pl.semaphore_wait(barrier, n - 1)
+    lax.fori_loop(0, n - 1, start_gather, 0)
     for load in loads:
         load.wait()
     lax.fori_loop(0, sub // WIDE, merge, 0)
-    pl.semaphore_wait(barrier, n - 1)
-    lax.fori_loop(0, n - 1, start_gather, 0)
 
     def settle(i, carry):
         for _, turned, straight, crossed in arrays:

time: 31.3 us -> 29.9 us (0.955)
  Pallas kernels: 27.8 us -> 26.4 us
    pallas_call x1, Pallas kernels: 27.8 us -> 26.4 us  [on_device(): pl.pallas_call(functools.partial(kernel, n), out_shape=jax.ShapeDtypeStru...]
where the time goes in v6:
time: 29.9 us; the launch traced here: 29.7 us
  Pallas kernels  26.4 us (88%)
  between operations  1.93 us (6%)
  local copies, waits for them, and re-layouts  1.33 us (4%)
    pallas_call x1, Pallas kernels, on_device(): pl.pallas_call(functools.partial(kernel, n), out_shape=jax.ShapeDtypeStru...  26.4 us
    reshape x1, local copies, waits for them, and re-layouts, on_device(): return (out[:lane_tiles].reshape(pairs), out[lane_tiles:].reshape(pairs))  1.33 us

profile of v6, /device:TPU:1, one launch (start us, length us, event | category | flops | bytes accessed | tf_op | source)
XLA Modules:
  0.0 29.7 jit_solution(15660871633070644543)
XLA Ops:
  1.9 26.4 %shard_map.131 = f32[8,128]{1,0:T(8,128)} custom-call(f32[4]{0:T(128)} %occ_ref.1, f32[1,1]{1,0:T(1,128)} %bitcast.13.omega_ref, s32[1,1]{1,0:T(1,128)} %bitcast.12.live_ref, s32[1,128]{1,0:T(1,128)} %bitcast.17, s32[1,128]{1,0:T(1,128)} %bitcast.18, s32[1,128]{1,0:T(1,128)} %bitcast.19, bf16[128,4096]{1,0:T(8,128)(2,1)} %blocks_hbm.1, ...), custom_call_target="tpu_custom_call" | custom-call | tf_op jit(solution)/shard_map/pallas_call | solution.py:326
  28.3 1.3 %slice_bitcast_fusion = (f32[512]{0:T(512)}, f32[512]{0:T(512)}) fusion(f32[8,128]{1,0:T(8,128)} %shard_map.131), kind=kLoop, calls=%fused_computation | loop fusion | bytes 8192 | tf_op jit(solution)/shard_map/reshape | solution.py:368
